TPU v7x, 32 devices: a whole 2x2x4 slice. The times are simulated.
32 devices in a mesh: gx: 4 (over x, core), gy: 8 (over z, y).
Axes of the slice: x: 2, y: 2, z: 4, core: 2. Of those that a mesh axis runs over, the one named last changes fastest.
Arguments:
- forcing: float32 [8, 8, 8, 4, 8, 128], P(None, None, None, 'gx', 'gy'), may hold values from -6 to 6
- coefficient: float32 [8, 8, 8, 4, 8, 128], P(None, None, None, 'gx', 'gy'), may hold values from 0.3 to 3
Outputs:
- pressure: float32 [8, 8, 8, 4, 8, 128], P(None, None, None, 'gx', 'gy')
- residual: float32 [8, 8, 8, 4, 8, 128], P(None, None, None, 'gx', 'gy')
All inputs are finite; a program needn't handle non-finite values.
Results may differ from a plain program's by a relative error of at most 0.0003.
Values sent between devices are 32-bit elements; how exact they have to be, the bound alone decides.
A program may use at most 64 MiB of HBM per device.

v0:
```python
import functools
import math

import jax
import jax.numpy as jnp
import numpy as np
from jax import lax
from jax.experimental import pallas as pl
from jax.experimental.pallas import tpu as pltpu
from jax.sharding import PartitionSpec as P

MESH = pl.DeviceIdType.MESH
stretch = (1.0, 64.0, 1.0)
DIRS = ((-1, 0), (1, 0), (0, -1), (0, 1), (-1, -1), (-1, 1), (1, -1), (1, 1))


def legendre_value(order, position):
    prev_value = 1.0
    this_value = position
    for degree_now in range(2, order + 1):
        next_value = (
            (2 * degree_now - 1) * position * this_value - (degree_now - 1) * prev_value
        ) / degree_now
        prev_value = this_value
        this_value = next_value
    return this_value


def gll_points():
    points = [-1.0]
    for node_index in range(1, 7):
        position = -math.cos(math.pi * node_index / 7.0)
        for newton_step in range(60):
            target = legendre_value(8, position) - legendre_value(6, position)
            slope = 15.0 * legendre_value(7, position)
            position = position - target / slope
        points.append(position)
    points.append(1.0)
    return points


def jacobi_eigen(matrix_in):
    order_n = len(matrix_in)
    work_mat = [list(one_row) for one_row in matrix_in]
    vectors = [
        [1.0 if row_index == col_index else 0.0 for col_index in range(order_n)]
        for row_index in range(order_n)
    ]
    for sweep_index in range(40):
        for first_idx in range(order_n):
            for second_idx in range(first_idx + 1, order_n):
                rotation = 0.5 * math.atan2(
                    2.0 * work_mat[first_idx][second_idx],
                    work_mat[second_idx][second_idx] - work_mat[first_idx][first_idx],
                )
                cosine = math.cos(rotation)
                sine_part = math.sin(rotation)
                for other in range(order_n):
                    left_val = work_mat[other][first_idx]
                    right_val = work_mat[other][second_idx]
                    work_mat[other][first_idx] = cosine * left_val - sine_part * right_val
                    work_mat[other][second_idx] = sine_part * left_val + cosine * right_val
                for other in range(order_n):
                    left_val = work_mat[first_idx][other]
                    right_val = work_mat[second_idx][other]
                    work_mat[first_idx][other] = cosine * left_val - sine_part * right_val
                    work_mat[second_idx][other] = sine_part * left_val + cosine * right_val
                for other in range(order_n):
                    left_val = vectors[other][first_idx]
                    right_val = vectors[other][second_idx]
                    vectors[other][first_idx] = cosine * left_val - sine_part * right_val
                    vectors[other][second_idx] = sine_part * left_val + cosine * right_val
    return ([work_mat[diag_index][diag_index] for diag_index in range(order_n)], vectors)


def spectral_tables():
    nodes = gll_points()
    values_at = [legendre_value(7, position) for position in nodes]
    weights = [2.0 / (56.0 * value_now * value_now) for value_now in values_at]
    derivative = np.zeros((8, 8))
    for row in range(8):
        for col in range(8):
            if row != col:
                derivative[row, col] = values_at[row] / (
                    values_at[col] * (nodes[row] - nodes[col])
                )
    derivative[0, 0] = -14.0
    derivative[7, 7] = 14.0
    weights = np.array(weights)
    stiffness = derivative.T @ np.diag(weights) @ derivative
    stiffness[0, 0] *= 2.0
    stiffness[7, 7] *= 2.0
    inv_root = 1.0 / np.sqrt(weights)
    symmetric = inv_root[:, None] * stiffness * inv_root[None, :]
    eigen_values, eigen_vectors = jacobi_eigen(symmetric.tolist())
    fdm_basis = inv_root[:, None] * np.array(eigen_vectors)
    nodes = np.array(nodes)
    hats = np.stack([(1.0 - nodes) / 2.0, (1.0 + nodes) / 2.0])
    return weights, derivative, fdm_basis, np.array(eigen_values), hats


def sine_table(cells):
    ids = np.arange(cells + 1)
    table = math.sqrt(2.0 / cells) * np.sin(math.pi * (np.outer(ids, ids) % (2 * cells)) / cells)
    table[0] = table[-1] = 0.0
    table[:, 0] = table[:, -1] = 0.0
    return table


def mode_values(cells):
    cosines = np.cos(math.pi * np.arange(1, cells) / cells)
    return (2.0 - 2.0 * cosines) / 2.0, 2.0 * (4.0 + 2.0 * cosines) / 6.0


def round_up(value, step):
    return -(-value // step) * step


def halves(table):
    table = np.asarray(table, np.float32)
    high = table.astype(jnp.bfloat16)
    low = (table - high.astype(np.float32)).astype(jnp.bfloat16)
    return np.concatenate([high, low], axis=0)


def pieces(table, count):
    table = np.asarray(table, np.float32)
    found = []
    for _ in range(count):
        found.append(table.astype(jnp.bfloat16))
        table = table - found[-1].astype(np.float32)
    return np.concatenate(found + [found[0]], axis=1)


def sixfold(table, axis):
    table = np.asarray(table, np.float32)
    found = []
    for _ in range(3):
        found.append(table.astype(jnp.bfloat16))
        table = table - found[-1].astype(np.float32)
    return np.concatenate([found[n] for n in (0, 1, 2, 0, 1, 0)], axis=axis)


def element_tables():
    weights, derivative, basis, eigen, hats = spectral_tables()
    eye = np.eye(8)
    cube = np.kron(np.kron(basis, basis), basis)
    total = (
        stretch[0] * eigen[:, None, None]
        + stretch[1] * eigen[None, :, None]
        + stretch[2] * eigen[None, None, :]
    ).reshape(-1)
    solve = (cube / total) @ cube.T
    along_j = np.kron(np.eye(4), np.kron(derivative, eye))
    along_k = np.kron(np.eye(4), np.kron(eye, derivative))
    forward = np.concatenate([along_j, along_k], axis=0)
    backward = np.concatenate([stretch[1] * along_j.T, stretch[2] * along_k.T], axis=1)
    corner = np.stack(
        [
            np.kron(np.kron(hats[a], hats[b]), hats[c])
            for c in range(2)
            for a in range(2)
            for b in range(2)
        ]
    )
    return weights, derivative, solve, forward, backward, corner


def coarse_tables(size_x, size_y, depth):
    sine_x, sine_y, sine_z = sine_table(size_x), sine_table(size_y), sine_table(depth)
    modes = (size_x - 1) * (size_y - 1)
    rows = round_up(modes + 2, 8)
    waves_y = size_y - 1
    rows_y = round_up(2 * waves_y + 2, 8)
    along_y = np.zeros((rows_y, size_y, 4))
    along_x = np.zeros((rows, size_x, rows_y))
    for a in range(2):
        for y in range(size_y):
            for b in range(2):
                along_y[a : 2 * waves_y : 2, y, 2 * a + b] = sine_y[1:-1, y + b]
        for x in range(size_x):
            for n in range(waves_y):
                along_x[n : modes : waves_y, x, 2 * n + a] = sine_x[1:-1, x + a]
    for q in range(2):
        along_y[2 * waves_y + q, :, q] = 1.0
        along_x[modes + q, :, 2 * waves_y + q] = 1.0
    stiff_x, mass_x = mode_values(size_x)
    stiff_y, mass_y = mode_values(size_y)
    stiff_z, mass_z = mode_values(depth)
    denominator = (
        stretch[0] * stiff_x[:, None, None] * mass_y[None, :, None] * mass_z[None, None, :]
        + stretch[1] * mass_x[:, None, None] * stiff_y[None, :, None] * mass_z[None, None, :]
        + stretch[2] * mass_x[:, None, None] * mass_y[None, :, None] * stiff_z[None, None, :]
    )
    inverse = np.zeros((rows, depth))
    inverse[:modes, 1:] = (1.0 / denominator).reshape(modes, depth - 1)
    back = np.zeros((size_x, size_y, 16, rows))
    for x in range(size_x):
        for y in range(size_y):
            for c in range(2):
                for a in range(2):
                    for b in range(2):
                        back[x, y, 4 * c + 2 * a + b, :modes] = np.outer(
                            sine_x[1:-1, x + a], sine_y[1:-1, y + b]
                        ).reshape(-1)
    return (
        along_y.reshape(rows_y, -1),
        along_x.reshape(rows, -1),
        inverse,
        back.reshape(size_x * size_y, 16, rows),
        sine_z[:depth, :depth],
    )


def parts(field):
    high = field.astype(jnp.bfloat16)
    return high, (field - high.astype(jnp.float32)).astype(jnp.bfloat16)


def both_dot(left, right):
    rows, lanes = left.shape[0], right.shape[1]
    sums = jnp.dot(
        jnp.concatenate(parts(left), axis=0),
        jnp.concatenate(parts(right), axis=1),
        preferred_element_type=jnp.float32,
    )
    return (sums[:rows, :lanes] + sums[rows:, :lanes]) + (sums[:rows, lanes:] + sums[rows:, lanes:])


def split_dot(table, field):
    lanes = field.shape[1]
    rows = table.shape[0] // 2
    high = field.astype(jnp.bfloat16)
    low = (field - high.astype(jnp.float32)).astype(jnp.bfloat16)
    both = jnp.concatenate([high, low], axis=1)
    top = jnp.dot(table[:rows], both, preferred_element_type=jnp.float32)
    bottom = jnp.dot(table[rows:], both, preferred_element_type=jnp.float32)
    return (top[:, :lanes] + bottom[:, :lanes]) + (top[:, lanes:] + bottom[:, lanes:])


def six_parts(value, axis):
    found = []
    for _ in range(3):
        found.append(value.astype(jnp.bfloat16).astype(jnp.float32))
        value = value - found[-1]
    order = [found[n] for n in (0, 0, 0, 1, 1, 2)]
    return jnp.concatenate(order, axis=axis).astype(jnp.bfloat16)


def table_dot(table, value):
    return jnp.dot(table, six_parts(value, 0), preferred_element_type=jnp.float32)


def dot_table(value, table):
    return jnp.dot(six_parts(value, 1), table, preferred_element_type=jnp.float32)


def wide_dot(table, field):
    high, low = parts(field)
    pieces = table.shape[1] // field.shape[0]
    return jnp.dot(
        table,
        jnp.concatenate([high] * (pieces - 1) + [low], axis=0),
        preferred_element_type=jnp.float32,
    )


def copy_kernel(p_in, r_in, p_out, r_out):
    p_out[...] = p_in[...]
    r_out[...] = r_in[...]


def kernel(size_x, size_y, weights, derivative, modes, *refs):
    n_in = 13
    inputs, (p_ref, r_ref) = refs[:n_in], refs[n_in : n_in + 2]
    local = refs[n_in + 2 : 2 * n_in + 2]
    (
        cw, out, base, first, second, image, alpha, beta_raw, smooth, flux_i,
        rx, ry, re, mine_y, got_y, mine_x, got_x, mine_s, got_s,
        in_sem, halo_send, halo_recv, y_send, y_recv, x_send, x_recv,
    ) = refs[2 * n_in + 2 :]
    (
        f_ref, corner_ref, coef_ref, weight_ref, solve_ref,
        forward_ref, backward_ref,
        along_y_ref, along_x_ref, sine_ref, inverse_ref, back_ref, spread_ref,
    ) = local
    lanes = f_ref.shape[2]
    my_x = lax.axis_index("gx")
    my_y = lax.axis_index("gy")
    me = my_x * size_y + my_y

    fetches = [
        pltpu.make_async_copy(
            inputs[n].at[me] if local[n] is back_ref else inputs[n], local[n], in_sem.at[n]
        )
        for n in range(n_in)
    ]
    for fetch in fetches:
        fetch.start()

    def exists(direction):
        dx, dy = direction
        ok = None
        for pos, size, step in ((my_x, size_x, dx), (my_y, size_y, dy)):
            if step:
                cond = pos > 0 if step < 0 else pos < size - 1
                ok = cond if ok is None else jnp.logical_and(ok, cond)
        return ok

    def peers_y():
        for offset in range(1, size_y):
            other = my_y + offset
            yield (my_x, jnp.where(other >= size_y, other - size_y, other))

    def peers_x():
        for offset in range(1, size_x):
            other = my_x + offset
            yield (jnp.where(other >= size_x, other - size_x, other), my_y)

    barrier = pltpu.get_barrier_semaphore()
    count = jnp.int32(size_x - 1 + size_y - 1)
    for direction in DIRS[4:]:
        here = exists(direction)

        @pl.when(here)
        def _(direction=direction):
            pl.semaphore_signal(
                barrier,
                inc=1,
                device_id=(my_x + direction[0], my_y + direction[1]),
                device_id_type=MESH,
            )

        count = count + here.astype(jnp.int32)
    for other in [*peers_y(), *peers_x()]:
        pl.semaphore_signal(barrier, inc=1, device_id=other, device_id_type=MESH)

    def node_rows(step):
        return 0 if step < 0 else 7

    def source(direction):
        dx, dy = direction
        if dy == 0:
            return out.at[node_rows(dx)]
        ys = pl.ds(8 * node_rows(dy), 8)
        if dx == 0:
            return out.at[:, ys]
        return out.at[node_rows(dx), ys]

    def landing(turn, index):
        if index < 2:
            return rx.at[turn, index]
        if index < 4:
            return ry.at[turn, index - 2]
        return re.at[turn, index - 4]

    def halo_copy(turn, index):
        direction = DIRS[index]
        opposite = DIRS.index((-direction[0], -direction[1]))
        return pltpu.make_async_remote_copy(
            src_ref=source(direction),
            dst_ref=landing(turn, opposite),
            send_sem=halo_send.at[turn, index],
            recv_sem=halo_recv.at[turn, opposite],
            device_id=(my_x + direction[0], my_y + direction[1]),
            device_id_type=MESH,
        )

    def halo_arrival(turn, index):
        direction = DIRS[index]
        return pltpu.make_async_remote_copy(
            src_ref=source(direction),
            dst_ref=landing(turn, index),
            send_sem=halo_send.at[turn, index],
            recv_sem=halo_recv.at[turn, index],
            device_id=(my_x + direction[0], my_y + direction[1]),
            device_id_type=MESH,
        )

    lane = lax.broadcasted_iota(jnp.int32, (8, 8, lanes), 2)

    def sum_depth(raw):
        out[...] = raw
        head = out[:, pl.ds(0, 8, stride=8), :]
        tail = out[:, pl.ds(7, 8, stride=8), :]
        from_tail = pltpu.roll(tail.reshape(64, lanes), 1, 1).reshape(8, 8, lanes)
        from_head = pltpu.roll(head.reshape(64, lanes), lanes - 1, 1).reshape(8, 8, lanes)
        out[:, pl.ds(0, 8, stride=8), :] = jnp.where(lane == 0, 0.0, head + from_tail)
        out[:, pl.ds(7, 8, stride=8), :] = jnp.where(lane == lanes - 1, 0.0, tail + from_head)

    def send_halo(turn):
        for index in (2, 3, 4, 5, 6, 7, 0, 1):
            @pl.when(exists(DIRS[index]))
            def _(index=index):
                halo_copy(turn, index).start()

    def take_halo(turn, target):
        for index in range(8):
            @pl.when(exists(DIRS[index]))
            def _(index=index):
                halo_copy(turn, index).wait_send()
                halo_arrival(turn, index).wait_recv()

        has = [exists(direction) for direction in DIRS[:4]]
        target[pl.ds(1, 6), pl.ds(8, 48)] = out[pl.ds(1, 6), pl.ds(8, 48)]
        for side in range(2):
            i = 7 * side
            target[i, pl.ds(8, 48)] = jnp.where(
                has[side], out[i, pl.ds(8, 48)] + rx[turn, side, pl.ds(8, 48)], 0.0
            )
            target[pl.ds(1, 6), pl.ds(8 * i, 8)] = jnp.where(
                has[2 + side],
                out[pl.ds(1, 6), pl.ds(8 * i, 8)] + ry[turn, side, pl.ds(1, 6)],
                0.0,
            )
            for other in range(2):
                j = 7 * other
                target[i, pl.ds(8 * j, 8)] = jnp.where(
                    jnp.logical_and(has[side], has[2 + other]),
                    (out[i, pl.ds(8 * j, 8)] + rx[turn, side, pl.ds(8 * j, 8)])
                    + (ry[turn, other, i] + re[turn, 2 * side + other]),
                    0.0,
                )

    def send_to(peers, me_there, message, got, send, recv, value):
        message[...] = value
        got[me_there] = value
        for other in peers:
            pltpu.make_async_remote_copy(
                src_ref=message,
                dst_ref=got.at[me_there],
                send_sem=send,
                recv_sem=recv,
                device_id=other,
                device_id_type=MESH,
            ).start()

    def take_from(size, got, send, recv):
        span = got.at[pl.ds(0, size - 1)]
        copy = pltpu.make_async_remote_copy(
            src_ref=span,
            dst_ref=span,
            send_sem=send,
            recv_sem=recv,
            device_id=(jnp.where(my_x == 0, 1, 0), my_y),
            device_id_type=MESH,
        )
        copy.wait_send()
        copy.wait_recv()
        return got[...]

    def send_y(turn, value):
        send_to(
            peers_y(), my_y, mine_y.at[turn], got_y.at[turn],
            y_send.at[turn], y_recv.at[turn], value,
        )

    def take_y(turn):
        return take_from(size_y, got_y.at[turn], y_send.at[turn], y_recv.at[turn])

    def send_x(turn, value):
        mine, got = (mine_s, got_s) if turn == 2 else (mine_x.at[turn], got_x.at[turn])
        send_to(peers_x(), my_x, mine, got, x_send.at[turn], x_recv.at[turn], value)

    def take_x(turn):
        got = got_s if turn == 2 else got_x.at[turn]
        return take_from(size_x, got, x_send.at[turn], x_recv.at[turn])

    def pass_on(turn):
        send_x(turn, table_dot(along_y_ref[...], take_y(turn).reshape(size_y * 4, lanes)))

    row = lax.broadcasted_iota(jnp.int32, (8, lanes), 0)
    row4 = lax.broadcasted_iota(jnp.int32, (4, lanes), 0)
    lane4 = lax.broadcasted_iota(jnp.int32, (4, lanes), 1)

    def corner_message(raw):
        corners = both_dot(corner_ref[...], raw)
        moved = pltpu.roll(pltpu.roll(corners, 1, 1), 4, 0)
        return (corners + moved)[:4]

    def coarse_values(turn):
        gathered = take_x(turn)
        gathered = gathered.reshape(size_x * gathered.shape[1], lanes)
        combined = table_dot(along_x_ref[...], gathered)
        spectral = dot_table(combined, sine_ref[...]) * inverse_ref[...]
        mine = table_dot(back_ref[...], spectral)[:8]
        columns = dot_table(mine, sine_ref[...])
        corners = jnp.where(row < 4, columns, pltpu.roll(columns, lanes - 1, 1))
        return table_dot(spread_ref[...], corners), combined

    def local_solve(field):
        return split_dot(solve_ref[...], field).reshape(8, 64, lanes)

    def fluxes(field_ref):
        values = field_ref[...] - field_ref[:, pl.ds(27, 1)]
        grads = wide_dot(
            forward_ref[...],
            jnp.concatenate(
                [values[:4].reshape(256, lanes), values[4:].reshape(256, lanes)], axis=1
            ),
        )
        factor = jnp.concatenate(
            [cw[pl.ds(0, 4)].reshape(256, lanes), cw[pl.ds(4, 4)].reshape(256, lanes)], axis=1
        )
        grads_j, grads_k = grads[:256], grads[256:]
        flux_j, flux_k = grads_j * factor, grads_k * factor
        energy = stretch[1] * (grads_j * flux_j) + stretch[2] * (grads_k * flux_k)
        energy = jnp.sum(energy.reshape(32, 8, 2 * lanes), axis=0)
        energy = energy[:, :lanes] + energy[:, lanes:]
        for part in range(8):
            span = pl.ds(8 * part, 8)
            nodal = [field_ref[i, span] for i in range(8)]
            for p in range(8):
                grad = nodal[0] * derivative[p][0]
                for i in range(1, 8):
                    grad = grad + nodal[i] * derivative[p][i]
                flux = grad * cw[p, span]
                flux_i[p, span] = flux
                energy = energy + grad * flux
        return jnp.concatenate([flux_j, flux_k], axis=0), energy

    def divergence(flux, target):
        result = wide_dot(backward_ref[...], flux)
        for part in range(8):
            span = pl.ds(8 * part, 8)
            flux = [flux_i[p, span] for p in range(8)]
            for i in range(8):
                first_row = 64 * (i % 4) + 8 * part
                first_lane = lanes * (i // 4)
                total = result[first_row : first_row + 8, first_lane : first_lane + lanes]
                for p in range(8):
                    total = total + flux[p] * derivative[p][i]
                target[i, span] = total

    def partial(left, right):
        return jnp.sum((left * right).reshape(64, 8, lanes), axis=0)

    def row_sum(tile):
        return jnp.sum(tile, axis=0, keepdims=True)

    def total(rows):
        return jnp.sum(rows, axis=(0, 1), keepdims=True)

    fetches[0].wait()
    sum_depth(f_ref[...])
    pl.semaphore_wait(barrier, count)
    send_halo(0)
    fetches[1].wait()
    send_y(0, corner_message(f_ref[...].reshape(512, lanes)))
    fetches[2].wait()
    fetches[3].wait()
    for i in range(8):
        cw[i] = coef_ref[i] * (weight_ref[...] * weights[i])
    fetches[4].wait()
    take_halo(0, base)
    for fetch in fetches[5:]:
        fetch.wait()

    sum_depth(local_solve(base[...].reshape(512, lanes)))
    send_halo(1)
    pass_on(0)
    coarse, _ = coarse_values(0)
    take_halo(1, first)
    first[...] += coarse.reshape(8, 64, lanes)

    flux, curve = fluxes(first)
    divergence(flux, alpha)
    sum_depth(alpha[...])
    send_halo(2)
    message = corner_message(alpha[...].reshape(512, lanes))
    energy = total(partial(f_ref[...], first[...]))
    curve = total(curve)
    message = jnp.where(
        lane4 == 0, jnp.where(row4 == 0, energy, jnp.where(row4 == 1, curve, 0.0)), message
    )
    send_y(1, message)
    take_halo(2, image)

    sum_depth(local_solve(image[...].reshape(512, lanes)))
    send_halo(3)
    pass_on(1)
    coarse, combined = coarse_values(1)
    energy = combined[modes : modes + 1, 0:1]
    curve = combined[modes + 1 : modes + 2, 0:1]
    step = energy / curve
    take_halo(3, smooth)
    step3 = step.reshape(1, 1, 1)
    second[...] = first[...] - step3 * (smooth[...] + coarse.reshape(8, 64, lanes))

    fresh = row_sum(partial(f_ref[...] - step3 * alpha[...], second[...]))
    cross = row_sum(partial(alpha[...], second[...]))
    flux, along = fluxes(second)
    along = row_sum(along)
    send_y(
        2,
        jnp.where(
            row4 == 0, fresh, jnp.where(row4 == 1, along, jnp.where(row4 == 2, cross, 0.0))
        ),
    )
    divergence(flux, beta_raw)
    sum_depth(beta_raw[...])
    send_halo(4)
    send_x(2, jnp.sum(take_y(2), axis=0))
    take_halo(4, smooth)
    sums = jnp.sum(take_x(2), axis=0)
    fresh = total(sums[0:1])
    ratio = fresh / energy
    along = total(sums[1:2]) + 2.0 * ratio * total(sums[2:3]) + ratio * ratio * curve
    second_step = fresh / along
    ratio3 = ratio.reshape(1, 1, 1)
    second3 = second_step.reshape(1, 1, 1)
    p_ref[...] = step3 * first[...] + second3 * (second[...] + ratio3 * first[...])
    r_ref[...] = (base[...] - step3 * image[...]) - second3 * (smooth[...] + ratio3 * image[...])


def solution(mesh):
    size_x, size_y = mesh.shape["gx"], mesh.shape["gy"]
    weights, derivative, solve, forward, backward, corner = element_tables()
    spec = P(None, None, None, "gx", "gy", None)

    def on_device(forcing, coefficient):
        shape = forcing.shape
        depth = shape[5]
        along_y, along_x, inverse, back, sine = coarse_tables(size_x, size_y, depth)
        modes = (size_x - 1) * (size_y - 1)
        plane = np.outer(weights, weights).reshape(64, 1) * np.ones((1, depth))
        field = (8, 64, depth)
        operands = [
            forcing.reshape(field),
            np.asarray(corner, np.float32),
            coefficient.reshape(field),
            np.asarray(plane, np.float32),
            halves(solve),
            pieces(forward, 3),
            pieces(backward, 2),
            sixfold(along_y, 1),
            sixfold(along_x, 1),
            sixfold(sine, 0),
            np.asarray(inverse, np.float32),
            sixfold(back, 2),
            sixfold(corner.T, 1),
        ]
        shapes = [op.shape for op in operands]
        shapes[11] = shapes[11][1:]
        rows_y = along_y.shape[0]
        vmem = pl.BlockSpec(memory_space=pltpu.VMEM)
        pressure, residual = pl.pallas_call(
            functools.partial(
                kernel, size_x, size_y, weights.tolist(), derivative.tolist(), modes
            ),
            out_shape=[jax.ShapeDtypeStruct(field, jnp.float32)] * 2,
            in_specs=[pl.BlockSpec(memory_space=pltpu.HBM)] * len(operands),
            out_specs=[vmem, vmem],
            scratch_shapes=[pltpu.VMEM(dims, op.dtype) for dims, op in zip(shapes, operands)]
            + [pltpu.VMEM(field, jnp.float32)] * 10
            + [
                pltpu.VMEM((5, 2, 64, depth), jnp.float32),
                pltpu.VMEM((5, 2, 8, 8, depth), jnp.float32),
                pltpu.VMEM((5, 4, 8, depth), jnp.float32),
                pltpu.VMEM((3, 4, depth), jnp.float32),
                pltpu.VMEM((3, size_y, 4, depth), jnp.float32),
                pltpu.VMEM((2, rows_y, depth), jnp.float32),
                pltpu.VMEM((2, size_x, rows_y, depth), jnp.float32),
                pltpu.VMEM((4, depth), jnp.float32),
                pltpu.VMEM((size_x, 4, depth), jnp.float32),
                pltpu.SemaphoreType.DMA((len(operands),)),
                pltpu.SemaphoreType.DMA((5, 8)),
                pltpu.SemaphoreType.DMA((5, 8)),
                pltpu.SemaphoreType.DMA((3,)),
                pltpu.SemaphoreType.DMA((3,)),
                pltpu.SemaphoreType.DMA((3,)),
                pltpu.SemaphoreType.DMA((3,)),
            ],
            compiler_params=pltpu.CompilerParams(
                collective_id=0, has_side_effects=True, vmem_limit_bytes=60 * 1024 * 1024
            ),
        )(*operands)
        pressure, residual = pl.pallas_call(
            copy_kernel,
            out_shape=[jax.ShapeDtypeStruct(field, jnp.float32)] * 2,
            in_specs=[vmem, vmem],
            out_specs=[vmem, vmem],
            compiler_params=pltpu.CompilerParams(vmem_limit_bytes=60 * 1024 * 1024),
        )(pressure, residual)
        return pressure.reshape(shape), residual.reshape(shape)

    return jax.shard_map(
        on_device, mesh=mesh, in_specs=(spec, spec), out_specs=(spec, spec), check_vma=False
    )
```

profile of v0, /device:TPU:0, one launch (start us, length us, event | category | flops | bytes accessed | tf_op | source)
XLA Modules:
  0.0 35.5 jit_solution(3828450793831725073)
XLA Ops:
  0.6 33.1 %shard_map.140 = (f32[8,64,128]{2,1,0:T(8,128)}, f32[8,64,128]{2,1,0:T(8,128)}) custom-call(f32[8,64,128]{2,1,0:T(8,128)} %bitcast.8, f32[8,512]{1,0:T(8,128)} %constant.22.clone.refs_1_, f32[8,64,128]{2,1,0:T(8,128)} %bitcast.9, f32[64,128]{1,0:T(8,128)} %constant.23.clone.refs_3_, bf16[1024,512]{1,0:T(8,128)(2,1)} %constant.24.clone.refs_4_, ...), custom_call_target="tpu_custom_call" | custom-call | tf_op jit(solution)/shard_map/pallas_call | solution.py:647
  33.7 1.8 %shard_map.141 = (f32[8,64,128]{2,1,0:T(8,128)}, f32[8,64,128]{2,1,0:T(8,128)}) custom-call(f32[8,64,128]{2,1,0:T(8,128)} %get-tuple-element.6.p_in, f32[8,64,128]{2,1,0:T(8,128)} %get-tuple-element.7.r_in), custom_call_target="tpu_custom_call" | custom-call | tf_op jit(solution)/shard_map/pallas_call | solution.py:678
where the time goes:
time: 35.7 us; the launch traced here: 35.5 us
  Pallas kernels  34.9 us (98%)
  between operations  0.64 us (2%)
    pallas_call x1, Pallas kernels, on_device(): pl.pallas_call(functools.partial(kernel, size_x, size_y, weights.tolist()...  33.1 us
    pallas_call x1, Pallas kernels, on_device(): pl.pallas_call(copy_kernel, out_shape=[jax.ShapeDtypeStruct(field, jnp.fl...  1.84 us

commit v1 on v0

--- a/solution.py
+++ b/solution.py
@@ -163,7 +163,18 @@
             for b in range(2)
         ]
     )
-    return weights, derivative, solve, forward, backward, corner
+    node = np.arange(512).reshape(8, 8, 8)
+    faces = [node[:, 0], node[:, 7], node[0], node[7]]
+    solve_faces = solve[np.stack(faces).reshape(-1)]
+    solve_inner = solve[node[1:7, 1:7].reshape(-1)]
+    node = node[:4]
+    outer = [node[:, [0, 7]], node[[0, 3], 1:7]]
+    backward_outer = backward[np.concatenate([rows.reshape(-1) for rows in outer])]
+    backward_inner = backward[node[1:3, 1:7].reshape(-1)]
+    return (
+        weights, derivative, solve_faces, solve_inner,
+        forward, backward_outer, backward_inner, corner,
+    )
 
 
 def coarse_tables(size_x, size_y, depth):
@@ -271,17 +282,17 @@
 
 
 def kernel(size_x, size_y, weights, derivative, modes, *refs):
-    n_in = 13
+    n_in = 15
     inputs, (p_ref, r_ref) = refs[:n_in], refs[n_in : n_in + 2]
     local = refs[n_in + 2 : 2 * n_in + 2]
     (
-        cw, out, base, first, second, image, alpha, beta_raw, smooth, flux_i,
+        cw, faces, base, first, second, image, alpha, beta_raw, smooth, flux_i,
         rx, ry, re, mine_y, got_y, mine_x, got_x, mine_s, got_s,
         in_sem, halo_send, halo_recv, y_send, y_recv, x_send, x_recv,
     ) = refs[2 * n_in + 2 :]
     (
-        f_ref, corner_ref, coef_ref, weight_ref, solve_ref,
-        forward_ref, backward_ref,
+        f_ref, corner_ref, coef_ref, weight_ref, solve_faces_ref, solve_inner_ref,
+        forward_ref, backward_outer_ref, backward_inner_ref,
         along_y_ref, along_x_ref, sine_ref, inverse_ref, back_ref, spread_ref,
     ) = local
     lanes = f_ref.shape[2]
@@ -341,11 +352,10 @@
     def source(direction):
         dx, dy = direction
         if dy == 0:
-            return out.at[node_rows(dx)]
-        ys = pl.ds(8 * node_rows(dy), 8)
+            return faces.at[2 + (dx > 0)]
         if dx == 0:
-            return out.at[:, ys]
-        return out.at[node_rows(dx), ys]
+            return faces.at[int(dy > 0)]
+        return faces.at[2 + (dx > 0), pl.ds(8 * node_rows(dy), 8)]
 
     def landing(turn, index):
         if index < 2:
@@ -377,16 +387,27 @@
             device_id_type=MESH,
         )
 
-    lane = lax.broadcasted_iota(jnp.int32, (8, 8, lanes), 2)
-
-    def sum_depth(raw):
-        out[...] = raw
-        head = out[:, pl.ds(0, 8, stride=8), :]
-        tail = out[:, pl.ds(7, 8, stride=8), :]
-        from_tail = pltpu.roll(tail.reshape(64, lanes), 1, 1).reshape(8, 8, lanes)
-        from_head = pltpu.roll(head.reshape(64, lanes), lanes - 1, 1).reshape(8, 8, lanes)
-        out[:, pl.ds(0, 8, stride=8), :] = jnp.where(lane == 0, 0.0, head + from_tail)
-        out[:, pl.ds(7, 8, stride=8), :] = jnp.where(lane == lanes - 1, 0.0, tail + from_head)
+    def sum_depth(ref):
+        count = ref.shape[0]
+        lane = lax.broadcasted_iota(jnp.int32, (count, 8, lanes), 2)
+        head = ref[:, pl.ds(0, 8, stride=8), :]
+        tail = ref[:, pl.ds(7, 8, stride=8), :]
+        rows = (8 * count, lanes)
+        from_tail = pltpu.roll(tail.reshape(rows), 1, 1).reshape(lane.shape)
+        from_head = pltpu.roll(head.reshape(rows), lanes - 1, 1).reshape(lane.shape)
+        ref[:, pl.ds(0, 8, stride=8), :] = jnp.where(lane == 0, 0.0, head + from_tail)
+        ref[:, pl.ds(7, 8, stride=8), :] = jnp.where(lane == lanes - 1, 0.0, tail + from_head)
+
+    def send_faces(turn, raw_ref):
+        for side in range(2):
+            faces[side] = raw_ref[:, pl.ds(56 * side, 8)].reshape(64, lanes)
+            faces[2 + side] = raw_ref[7 * side]
+        sum_depth(faces)
+        send_halo(turn)
+
+    def fill_inner(target, raw):
+        target[pl.ds(1, 6), pl.ds(8, 48)] = raw
+        sum_depth(target)
 
     def send_halo(turn):
         for index in (2, 3, 4, 5, 6, 7, 0, 1):
@@ -402,23 +423,24 @@
                 halo_arrival(turn, index).wait_recv()
 
         has = [exists(direction) for direction in DIRS[:4]]
-        target[pl.ds(1, 6), pl.ds(8, 48)] = out[pl.ds(1, 6), pl.ds(8, 48)]
         for side in range(2):
             i = 7 * side
             target[i, pl.ds(8, 48)] = jnp.where(
-                has[side], out[i, pl.ds(8, 48)] + rx[turn, side, pl.ds(8, 48)], 0.0
+                has[side],
+                faces[2 + side, pl.ds(8, 48)] + rx[turn, side, pl.ds(8, 48)],
+                0.0,
             )
             target[pl.ds(1, 6), pl.ds(8 * i, 8)] = jnp.where(
                 has[2 + side],
-                out[pl.ds(1, 6), pl.ds(8 * i, 8)] + ry[turn, side, pl.ds(1, 6)],
+                faces[side, pl.ds(8, 48)] + ry[turn, side, pl.ds(8, 48)],
                 0.0,
-            )
+            ).reshape(6, 8, lanes)
             for other in range(2):
                 j = 7 * other
                 target[i, pl.ds(8 * j, 8)] = jnp.where(
                     jnp.logical_and(has[side], has[2 + other]),
-                    (out[i, pl.ds(8 * j, 8)] + rx[turn, side, pl.ds(8 * j, 8)])
-                    + (ry[turn, other, i] + re[turn, 2 * side + other]),
+                    (faces[2 + side, pl.ds(8 * j, 8)] + rx[turn, side, pl.ds(8 * j, 8)])
+                    + (ry[turn, other, pl.ds(8 * i, 8)] + re[turn, 2 * side + other]),
                     0.0,
                 )
 
@@ -488,8 +510,13 @@
         corners = jnp.where(row < 4, columns, pltpu.roll(columns, lanes - 1, 1))
         return table_dot(spread_ref[...], corners), combined
 
-    def local_solve(field):
-        return split_dot(solve_ref[...], field).reshape(8, 64, lanes)
+    def solve_and_send(turn, field):
+        faces[...] = split_dot(solve_faces_ref[...], field).reshape(4, 64, lanes)
+        sum_depth(faces)
+        send_halo(turn)
+
+    def solve_inner(field, target):
+        fill_inner(target, split_dot(solve_inner_ref[...], field).reshape(6, 48, lanes))
 
     def fluxes(field_ref):
         values = field_ref[...] - field_ref[:, pl.ds(27, 1)]
@@ -519,18 +546,38 @@
                 energy = energy + grad * flux
         return jnp.concatenate([flux_j, flux_k], axis=0), energy
 
-    def divergence(flux, target):
-        result = wide_dot(backward_ref[...], flux)
-        for part in range(8):
-            span = pl.ds(8 * part, 8)
-            flux = [flux_i[p, span] for p in range(8)]
+    def divergence(flux, target, tiles, product, place):
+        for j in range(8):
+            span = pl.ds(8 * j, 8)
+            along_i = [flux_i[p, span] for p in range(8)]
             for i in range(8):
-                first_row = 64 * (i % 4) + 8 * part
-                first_lane = lanes * (i // 4)
-                total = result[first_row : first_row + 8, first_lane : first_lane + lanes]
+                if (i, j) not in tiles:
+                    continue
+                row_at, lane_at = place(i % 4, j), lanes * (i // 4)
+                total = product[row_at : row_at + 8, lane_at : lane_at + lanes]
                 for p in range(8):
-                    total = total + flux[p] * derivative[p][i]
+                    total = total + along_i[p] * derivative[p][i]
                 target[i, span] = total
+
+    all_tiles = [(i, j) for i in range(8) for j in range(8)]
+    inner_tiles = [(i, j) for i, j in all_tiles if 0 < i < 7 and 0 < j < 7]
+    face_tiles = [tile for tile in all_tiles if tile not in inner_tiles]
+
+    def outer_place(i, j):
+        if j in (0, 7):
+            return 8 * (2 * i + (j == 7))
+        return 64 + 8 * (6 * (i == 3) + j - 1)
+
+    def operate(turn, flux, raw, target):
+        outer = wide_dot(backward_outer_ref[...], flux)
+        divergence(flux, raw, face_tiles, outer, outer_place)
+        send_faces(turn, raw)
+        middle = wide_dot(backward_inner_ref[...], flux)
+        ends = [(i, j) for i, j in inner_tiles if i in (3, 4)]
+        rest = [(i, j) for i, j in inner_tiles if i not in (3, 4)]
+        divergence(flux, raw, ends, outer, outer_place)
+        divergence(flux, raw, rest, middle, lambda i, j: 8 * (6 * (i - 1) + j - 1))
+        fill_inner(target, raw[pl.ds(1, 6), pl.ds(8, 48)])
 
     def partial(left, right):
         return jnp.sum((left * right).reshape(64, 8, lanes), axis=0)
@@ -542,31 +589,30 @@
         return jnp.sum(rows, axis=(0, 1), keepdims=True)
 
     fetches[0].wait()
-    sum_depth(f_ref[...])
     pl.semaphore_wait(barrier, count)
-    send_halo(0)
+    send_faces(0, f_ref)
     fetches[1].wait()
     send_y(0, corner_message(f_ref[...].reshape(512, lanes)))
+    fill_inner(base, f_ref[pl.ds(1, 6), pl.ds(8, 48)])
     fetches[2].wait()
     fetches[3].wait()
     for i in range(8):
         cw[i] = coef_ref[i] * (weight_ref[...] * weights[i])
     fetches[4].wait()
     take_halo(0, base)
+
+    field = base[...].reshape(512, lanes)
+    solve_and_send(1, field)
     for fetch in fetches[5:]:
         fetch.wait()
-
-    sum_depth(local_solve(base[...].reshape(512, lanes)))
-    send_halo(1)
     pass_on(0)
+    solve_inner(field, first)
     coarse, _ = coarse_values(0)
     take_halo(1, first)
     first[...] += coarse.reshape(8, 64, lanes)
 
     flux, curve = fluxes(first)
-    divergence(flux, alpha)
-    sum_depth(alpha[...])
-    send_halo(2)
+    operate(2, flux, alpha, image)
     message = corner_message(alpha[...].reshape(512, lanes))
     energy = total(partial(f_ref[...], first[...]))
     curve = total(curve)
@@ -576,15 +622,16 @@
     send_y(1, message)
     take_halo(2, image)
 
-    sum_depth(local_solve(image[...].reshape(512, lanes)))
-    send_halo(3)
+    field = image[...].reshape(512, lanes)
+    solve_and_send(3, field)
     pass_on(1)
+    solve_inner(field, smooth)
     coarse, combined = coarse_values(1)
     energy = combined[modes : modes + 1, 0:1]
     curve = combined[modes + 1 : modes + 2, 0:1]
     step = energy / curve
+    step3 = step.reshape(1, 1, 1)
     take_halo(3, smooth)
-    step3 = step.reshape(1, 1, 1)
     second[...] = first[...] - step3 * (smooth[...] + coarse.reshape(8, 64, lanes))
 
     fresh = row_sum(partial(f_ref[...] - step3 * alpha[...], second[...]))
@@ -597,9 +644,7 @@
             row4 == 0, fresh, jnp.where(row4 == 1, along, jnp.where(row4 == 2, cross, 0.0))
         ),
     )
-    divergence(flux, beta_raw)
-    sum_depth(beta_raw[...])
-    send_halo(4)
+    operate(4, flux, beta_raw, smooth)
     send_x(2, jnp.sum(take_y(2), axis=0))
     take_halo(4, smooth)
     sums = jnp.sum(take_x(2), axis=0)
@@ -615,7 +660,10 @@
 
 def solution(mesh):
     size_x, size_y = mesh.shape["gx"], mesh.shape["gy"]
-    weights, derivative, solve, forward, backward, corner = element_tables()
+    (
+        weights, derivative, solve_faces, solve_inner,
+        forward, backward_outer, backward_inner, corner,
+    ) = element_tables()
     spec = P(None, None, None, "gx", "gy", None)
 
     def on_device(forcing, coefficient):
@@ -630,9 +678,11 @@
             np.asarray(corner, np.float32),
             coefficient.reshape(field),
             np.asarray(plane, np.float32),
-            halves(solve),
+            halves(solve_faces),
+            halves(solve_inner),
             pieces(forward, 3),
-            pieces(backward, 2),
+            pieces(backward_outer, 2),
+            pieces(backward_inner, 2),
             sixfold(along_y, 1),
             sixfold(along_x, 1),
             sixfold(sine, 0),
@@ -641,7 +691,7 @@
             sixfold(corner.T, 1),
         ]
         shapes = [op.shape for op in operands]
-        shapes[11] = shapes[11][1:]
+        shapes[13] = shapes[13][1:]
         rows_y = along_y.shape[0]
         vmem = pl.BlockSpec(memory_space=pltpu.VMEM)
         pressure, residual = pl.pallas_call(
@@ -652,10 +702,12 @@
             in_specs=[pl.BlockSpec(memory_space=pltpu.HBM)] * len(operands),
             out_specs=[vmem, vmem],
             scratch_shapes=[pltpu.VMEM(dims, op.dtype) for dims, op in zip(shapes, operands)]
-            + [pltpu.VMEM(field, jnp.float32)] * 10
+            + [pltpu.VMEM(field, jnp.float32)]
+            + [pltpu.VMEM((4, 64, depth), jnp.float32)]
+            + [pltpu.VMEM(field, jnp.float32)] * 8
             + [
                 pltpu.VMEM((5, 2, 64, depth), jnp.float32),
-                pltpu.VMEM((5, 2, 8, 8, depth), jnp.float32),
+                pltpu.VMEM((5, 2, 64, depth), jnp.float32),
                 pltpu.VMEM((5, 4, 8, depth), jnp.float32),
                 pltpu.VMEM((3, 4, depth), jnp.float32),
                 pltpu.VMEM((3, size_y, 4, depth), jnp.float32),

time: 35.7 us -> 35.5 us (level)
  no operation moved by 1% of the time
where the time goes in v1:
time: 35.5 us; the launch traced here: 35.4 us
  Pallas kernels  34.7 us (98%)
  between operations  0.64 us (2%)
    pallas_call x1, Pallas kernels, on_device(): pl.pallas_call(functools.partial(kernel, size_x, size_y, weights.tolist()...  32.9 us
    pallas_call x1, Pallas kernels, on_device(): pl.pallas_call(copy_kernel, out_shape=[jax.ShapeDtypeStruct(field, jnp.fl...  1.84 us

profile of v1, /device:TPU:0, one launch (start us, length us, event | category | flops | bytes accessed | tf_op | source)
XLA Modules:
  0.0 35.4 jit_solution(4978409270047724031)
XLA Ops:
  0.6 32.9 %shard_map.158 = (f32[8,64,128]{2,1,0:T(8,128)}, f32[8,64,128]{2,1,0:T(8,128)}) custom-call(f32[8,64,128]{2,1,0:T(8,128)} %bitcast.8, f32[8,512]{1,0:T(8,128)} %constant.26.clone.refs_1_, f32[8,64,128]{2,1,0:T(8,128)} %bitcast.9, f32[64,128]{1,0:T(8,128)} %constant.27.clone.refs_3_, bf16[512,512]{1,0:T(8,128)(2,1)} %constant.28.clone.refs_4_, ...), custom_call_target="tpu_custom_call" | custom-call | tf_op jit(solution)/shard_map/pallas_call | solution.py:697
  33.5 1.8 %shard_map.159 = (f32[8,64,128]{2,1,0:T(8,128)}, f32[8,64,128]{2,1,0:T(8,128)}) custom-call(f32[8,64,128]{2,1,0:T(8,128)} %get-tuple-element.6.p_in, f32[8,64,128]{2,1,0:T(8,128)} %get-tuple-element.7.r_in), custom_call_target="tpu_custom_call" | custom-call | tf_op jit(solution)/shard_map/pallas_call | solution.py:730

commit v2 on v1

--- a/solution.py
+++ b/solution.py
@@ -288,7 +288,7 @@
     (
         cw, faces, base, first, second, image, alpha, beta_raw, smooth, flux_i,
         rx, ry, re, mine_y, got_y, mine_x, got_x, mine_s, got_s,
-        in_sem, halo_send, halo_recv, y_send, y_recv, x_send, x_recv,
+        in_sem, halo_send, halo_recv, y_send, y_recv, x_send, x_recv, s_send, s_recv,
     ) = refs[2 * n_in + 2 :]
     (
         f_ref, corner_ref, coef_ref, weight_ref, solve_faces_ref, solve_inner_ref,
@@ -327,6 +327,14 @@
         for offset in range(1, size_x):
             other = my_x + offset
             yield (jnp.where(other >= size_x, other - size_x, other), my_y)
+
+    def peers_all():
+        for offset_y in range(size_y - 1, -1, -1):
+            other_y = my_y + offset_y
+            other_y = jnp.where(other_y >= size_y, other_y - size_y, other_y)
+            for offset_x in range(0 if offset_y else 1, size_x):
+                other_x = my_x + offset_x
+                yield (jnp.where(other_x >= size_x, other_x - size_x, other_x), other_y)
 
     barrier = pltpu.get_barrier_semaphore()
     count = jnp.int32(size_x - 1 + size_y - 1)
@@ -481,12 +489,13 @@
         return take_from(size_y, got_y.at[turn], y_send.at[turn], y_recv.at[turn])
 
     def send_x(turn, value):
-        mine, got = (mine_s, got_s) if turn == 2 else (mine_x.at[turn], got_x.at[turn])
-        send_to(peers_x(), my_x, mine, got, x_send.at[turn], x_recv.at[turn], value)
+        send_to(
+            peers_x(), my_x, mine_x.at[turn], got_x.at[turn],
+            x_send.at[turn], x_recv.at[turn], value,
+        )
 
     def take_x(turn):
-        got = got_s if turn == 2 else got_x.at[turn]
-        return take_from(size_x, got, x_send.at[turn], x_recv.at[turn])
+        return take_from(size_x, got_x.at[turn], x_send.at[turn], x_recv.at[turn])
 
     def pass_on(turn):
         send_x(turn, table_dot(along_y_ref[...], take_y(turn).reshape(size_y * 4, lanes)))
@@ -568,7 +577,7 @@
             return 8 * (2 * i + (j == 7))
         return 64 + 8 * (6 * (i == 3) + j - 1)
 
-    def operate(turn, flux, raw, target):
+    def operate(turn, flux, raw, target, then=None):
         outer = wide_dot(backward_outer_ref[...], flux)
         divergence(flux, raw, face_tiles, outer, outer_place)
         send_faces(turn, raw)
@@ -577,6 +586,8 @@
         rest = [(i, j) for i, j in inner_tiles if i not in (3, 4)]
         divergence(flux, raw, ends, outer, outer_place)
         divergence(flux, raw, rest, middle, lambda i, j: 8 * (6 * (i - 1) + j - 1))
+        if then:
+            then()
         fill_inner(target, raw[pl.ds(1, 6), pl.ds(8, 48)])
 
     def partial(left, right):
@@ -611,15 +622,18 @@
     take_halo(1, first)
     first[...] += coarse.reshape(8, 64, lanes)
 
-    flux, curve = fluxes(first)
-    operate(2, flux, alpha, image)
-    message = corner_message(alpha[...].reshape(512, lanes))
-    energy = total(partial(f_ref[...], first[...]))
-    curve = total(curve)
-    message = jnp.where(
-        lane4 == 0, jnp.where(row4 == 0, energy, jnp.where(row4 == 1, curve, 0.0)), message
-    )
-    send_y(1, message)
+    flux, curve_part = fluxes(first)
+
+    def send_residual():
+        message = corner_message(alpha[...].reshape(512, lanes))
+        scalars = jnp.where(
+            row4 == 0,
+            total(partial(f_ref[...], first[...])),
+            jnp.where(row4 == 1, total(curve_part), 0.0),
+        )
+        send_y(1, jnp.where(lane4 == 0, scalars, message))
+
+    operate(2, flux, alpha, image, send_residual)
     take_halo(2, image)
 
     field = image[...].reshape(512, lanes)
@@ -638,16 +652,13 @@
     cross = row_sum(partial(alpha[...], second[...]))
     flux, along = fluxes(second)
     along = row_sum(along)
-    send_y(
-        2,
-        jnp.where(
-            row4 == 0, fresh, jnp.where(row4 == 1, along, jnp.where(row4 == 2, cross, 0.0))
-        ),
+    sums = jnp.where(
+        row4 == 0, fresh, jnp.where(row4 == 1, along, jnp.where(row4 == 2, cross, 0.0))
     )
+    send_to(peers_all(), me, mine_s, got_s, s_send, s_recv, sums)
     operate(4, flux, beta_raw, smooth)
-    send_x(2, jnp.sum(take_y(2), axis=0))
     take_halo(4, smooth)
-    sums = jnp.sum(take_x(2), axis=0)
+    sums = jnp.sum(take_from(size_x * size_y, got_s, s_send, s_recv), axis=0)
     fresh = total(sums[0:1])
     ratio = fresh / energy
     along = total(sums[1:2]) + 2.0 * ratio * total(sums[2:3]) + ratio * ratio * curve
@@ -709,19 +720,21 @@
                 pltpu.VMEM((5, 2, 64, depth), jnp.float32),
                 pltpu.VMEM((5, 2, 64, depth), jnp.float32),
                 pltpu.VMEM((5, 4, 8, depth), jnp.float32),
-                pltpu.VMEM((3, 4, depth), jnp.float32),
-                pltpu.VMEM((3, size_y, 4, depth), jnp.float32),
+                pltpu.VMEM((2, 4, depth), jnp.float32),
+                pltpu.VMEM((2, size_y, 4, depth), jnp.float32),
                 pltpu.VMEM((2, rows_y, depth), jnp.float32),
                 pltpu.VMEM((2, size_x, rows_y, depth), jnp.float32),
                 pltpu.VMEM((4, depth), jnp.float32),
-                pltpu.VMEM((size_x, 4, depth), jnp.float32),
+                pltpu.VMEM((size_x * size_y, 4, depth), jnp.float32),
                 pltpu.SemaphoreType.DMA((len(operands),)),
                 pltpu.SemaphoreType.DMA((5, 8)),
                 pltpu.SemaphoreType.DMA((5, 8)),
-                pltpu.SemaphoreType.DMA((3,)),
-                pltpu.SemaphoreType.DMA((3,)),
-                pltpu.SemaphoreType.DMA((3,)),
-                pltpu.SemaphoreType.DMA((3,)),
+                pltpu.SemaphoreType.DMA((2,)),
+                pltpu.SemaphoreType.DMA((2,)),
+                pltpu.SemaphoreType.DMA((2,)),
+                pltpu.SemaphoreType.DMA((2,)),
+                pltpu.SemaphoreType.DMA(()),
+                pltpu.SemaphoreType.DMA(()),
             ],
             compiler_params=pltpu.CompilerParams(
                 collective_id=0, has_side_effects=True, vmem_limit_bytes=60 * 1024 * 1024

time: 35.5 us -> 34.2 us (0.963)
  Pallas kernels: 34.7 us -> 33.5 us
    pallas_call x1, Pallas kernels: 32.9 us -> 31.6 us  [on_device(): pl.pallas_call(functools.partial(kernel, size_x, size_y, weights.tolist()...]
where the time goes in v2:
time: 34.2 us; the launch traced here: 34.1 us
  Pallas kernels  33.5 us (98%)
  between operations  0.64 us (2%)
    pallas_call x1, Pallas kernels, on_device(): pl.pallas_call(functools.partial(kernel, size_x, size_y, weights.tolist()...  31.6 us
    pallas_call x1, Pallas kernels, on_device(): pl.pallas_call(copy_kernel, out_shape=[jax.ShapeDtypeStruct(field, jnp.fl...  1.84 us

profile of v2, /device:TPU:0, one launch (start us, length us, event | category | flops | bytes accessed | tf_op | source)
XLA Modules:
  0.0 34.1 jit_solution(16377932640704057561)
XLA Ops:
  0.6 31.6 %shard_map.158 = (f32[8,64,128]{2,1,0:T(8,128)}, f32[8,64,128]{2,1,0:T(8,128)}) custom-call(f32[8,64,128]{2,1,0:T(8,128)} %bitcast.8, f32[8,512]{1,0:T(8,128)} %constant.26.clone.refs_1_, f32[8,64,128]{2,1,0:T(8,128)} %bitcast.9, f32[64,128]{1,0:T(8,128)} %constant.27.clone.refs_3_, bf16[512,512]{1,0:T(8,128)(2,1)} %constant.28.clone.refs_4_, ...), custom_call_target="tpu_custom_call" | custom-call | tf_op jit(solution)/shard_map/pallas_call | solution.py:708
  32.3 1.8 %shard_map.159 = (f32[8,64,128]{2,1,0:T(8,128)}, f32[8,64,128]{2,1,0:T(8,128)}) custom-call(f32[8,64,128]{2,1,0:T(8,128)} %get-tuple-element.6.p_in, f32[8,64,128]{2,1,0:T(8,128)} %get-tuple-element.7.r_in), custom_call_target="tpu_custom_call" | custom-call | tf_op jit(solution)/shard_map/pallas_call | solution.py:743

commit v3 on v2

--- a/solution.py
+++ b/solution.py
@@ -195,6 +195,16 @@
     for q in range(2):
         along_y[2 * waves_y + q, :, q] = 1.0
         along_x[modes + q, :, 2 * waves_y + q] = 1.0
+    direct = np.zeros((rows, size_x, size_y, 4))
+    for x in range(size_x):
+        for y in range(size_y):
+            for a in range(2):
+                for b in range(2):
+                    direct[:modes, x, y, 2 * a + b] = np.outer(
+                        sine_x[1:-1, x + a], sine_y[1:-1, y + b]
+                    ).reshape(-1)
+    for q in range(2):
+        direct[modes + q, :, :, q] = 1.0
     stiff_x, mass_x = mode_values(size_x)
     stiff_y, mass_y = mode_values(size_y)
     stiff_z, mass_z = mode_values(depth)
@@ -217,6 +227,7 @@
     return (
         along_y.reshape(rows_y, -1),
         along_x.reshape(rows, -1),
+        direct.reshape(rows, -1),
         inverse,
         back.reshape(size_x * size_y, 16, rows),
         sine_z[:depth, :depth],
@@ -282,18 +293,18 @@
 
 
 def kernel(size_x, size_y, weights, derivative, modes, *refs):
-    n_in = 15
+    n_in = 16
     inputs, (p_ref, r_ref) = refs[:n_in], refs[n_in : n_in + 2]
     local = refs[n_in + 2 : 2 * n_in + 2]
     (
         cw, faces, base, first, second, image, alpha, beta_raw, smooth, flux_i,
-        rx, ry, re, mine_y, got_y, mine_x, got_x, mine_s, got_s,
-        in_sem, halo_send, halo_recv, y_send, y_recv, x_send, x_recv, s_send, s_recv,
+        rx, ry, re, mine_y, got_y, mine_x, got_x, mine_s, got_s, mine_a, got_a,
+        in_sem, halo_send, halo_recv, y_send, y_recv, x_send, x_recv, s_send, s_recv, a_send, a_recv,
     ) = refs[2 * n_in + 2 :]
     (
         f_ref, corner_ref, coef_ref, weight_ref, solve_faces_ref, solve_inner_ref,
         forward_ref, backward_outer_ref, backward_inner_ref,
-        along_y_ref, along_x_ref, sine_ref, inverse_ref, back_ref, spread_ref,
+        along_y_ref, along_x_ref, direct_ref, sine_ref, inverse_ref, back_ref, spread_ref,
     ) = local
     lanes = f_ref.shape[2]
     my_x = lax.axis_index("gx")
@@ -510,9 +521,13 @@
         return (corners + moved)[:4]
 
     def coarse_values(turn):
-        gathered = take_x(turn)
-        gathered = gathered.reshape(size_x * gathered.shape[1], lanes)
-        combined = table_dot(along_x_ref[...], gathered)
+        if turn == 0:
+            gathered = take_x(turn)
+            gathered = gathered.reshape(size_x * gathered.shape[1], lanes)
+            combined = table_dot(along_x_ref[...], gathered)
+        else:
+            gathered = take_from(size_x * size_y, got_a, a_send, a_recv)
+            combined = table_dot(direct_ref[...], gathered.reshape(-1, lanes))
         spectral = dot_table(combined, sine_ref[...]) * inverse_ref[...]
         mine = table_dot(back_ref[...], spectral)[:8]
         columns = dot_table(mine, sine_ref[...])
@@ -631,14 +646,14 @@
             total(partial(f_ref[...], first[...])),
             jnp.where(row4 == 1, total(curve_part), 0.0),
         )
-        send_y(1, jnp.where(lane4 == 0, scalars, message))
+        message = jnp.where(lane4 == 0, scalars, message)
+        send_to(peers_all(), me, mine_a, got_a, a_send, a_recv, message)
 
     operate(2, flux, alpha, image, send_residual)
     take_halo(2, image)
 
     field = image[...].reshape(512, lanes)
     solve_and_send(3, field)
-    pass_on(1)
     solve_inner(field, smooth)
     coarse, combined = coarse_values(1)
     energy = combined[modes : modes + 1, 0:1]
@@ -680,7 +695,7 @@
     def on_device(forcing, coefficient):
         shape = forcing.shape
         depth = shape[5]
-        along_y, along_x, inverse, back, sine = coarse_tables(size_x, size_y, depth)
+        along_y, along_x, direct, inverse, back, sine = coarse_tables(size_x, size_y, depth)
         modes = (size_x - 1) * (size_y - 1)
         plane = np.outer(weights, weights).reshape(64, 1) * np.ones((1, depth))
         field = (8, 64, depth)
@@ -696,13 +711,14 @@
             pieces(backward_inner, 2),
             sixfold(along_y, 1),
             sixfold(along_x, 1),
+            sixfold(direct, 1),
             sixfold(sine, 0),
             np.asarray(inverse, np.float32),
             sixfold(back, 2),
             sixfold(corner.T, 1),
         ]
         shapes = [op.shape for op in operands]
-        shapes[13] = shapes[13][1:]
+        shapes[14] = shapes[14][1:]
         rows_y = along_y.shape[0]
         vmem = pl.BlockSpec(memory_space=pltpu.VMEM)
         pressure, residual = pl.pallas_call(
@@ -726,6 +742,8 @@
                 pltpu.VMEM((2, size_x, rows_y, depth), jnp.float32),
                 pltpu.VMEM((4, depth), jnp.float32),
                 pltpu.VMEM((size_x * size_y, 4, depth), jnp.float32),
+                pltpu.VMEM((4, depth), jnp.float32),
+                pltpu.VMEM((size_x * size_y, 4, depth), jnp.float32),
                 pltpu.SemaphoreType.DMA((len(operands),)),
                 pltpu.SemaphoreType.DMA((5, 8)),
                 pltpu.SemaphoreType.DMA((5, 8)),
@@ -733,6 +751,8 @@
                 pltpu.SemaphoreType.DMA((2,)),
                 pltpu.SemaphoreType.DMA((2,)),
                 pltpu.SemaphoreType.DMA((2,)),
+                pltpu.SemaphoreType.DMA(()),
+                pltpu.SemaphoreType.DMA(()),
                 pltpu.SemaphoreType.DMA(()),
                 pltpu.SemaphoreType.DMA(()),
             ],

time: 34.2 us -> 33.7 us (0.985)
  Pallas kernels: 33.5 us -> 33 us
    pallas_call x1, Pallas kernels: 31.6 us -> 31.1 us  [on_device(): pl.pallas_call(functools.partial(kernel, size_x, size_y, weights.tolist()...]
where the time goes in v3:
time: 33.7 us; the launch traced here: 33.6 us
  Pallas kernels  33 us (98%)
  between operations  0.64 us (2%)
    pallas_call x1, Pallas kernels, on_device(): pl.pallas_call(functools.partial(kernel, size_x, size_y, weights.tolist()...  31.1 us
    pallas_call x1, Pallas kernels, on_device(): pl.pallas_call(copy_kernel, out_shape=[jax.ShapeDtypeStruct(field, jnp.fl...  1.84 us

profile of v3, /device:TPU:0, one launch (start us, length us, event | category | flops | bytes accessed | tf_op | source)
XLA Modules:
  0.0 33.6 jit_solution(10147949722025015226)
XLA Ops:
  0.6 31.1 %shard_map.167 = (f32[8,64,128]{2,1,0:T(8,128)}, f32[8,64,128]{2,1,0:T(8,128)}) custom-call(f32[8,64,128]{2,1,0:T(8,128)} %bitcast.8, f32[8,512]{1,0:T(8,128)} %constant.28.clone.refs_1_, f32[8,64,128]{2,1,0:T(8,128)} %bitcast.9, f32[64,128]{1,0:T(8,128)} %constant.29.clone.refs_3_, bf16[512,512]{1,0:T(8,128)(2,1)} %constant.30.clone.refs_4_, ...), custom_call_target="tpu_custom_call" | custom-call | tf_op jit(solution)/shard_map/pallas_call | solution.py:724
  31.8 1.8 %shard_map.168 = (f32[8,64,128]{2,1,0:T(8,128)}, f32[8,64,128]{2,1,0:T(8,128)}) custom-call(f32[8,64,128]{2,1,0:T(8,128)} %get-tuple-element.6.p_in, f32[8,64,128]{2,1,0:T(8,128)} %get-tuple-element.7.r_in), custom_call_target="tpu_custom_call" | custom-call | tf_op jit(solution)/shard_map/pallas_call | solution.py:763

commit v4 on v3

--- a/solution.py
+++ b/solution.py
@@ -417,12 +417,11 @@
         ref[:, pl.ds(0, 8, stride=8), :] = jnp.where(lane == 0, 0.0, head + from_tail)
         ref[:, pl.ds(7, 8, stride=8), :] = jnp.where(lane == lanes - 1, 0.0, tail + from_head)
 
-    def send_faces(turn, raw_ref):
+    def load_faces(raw_ref):
         for side in range(2):
             faces[side] = raw_ref[:, pl.ds(56 * side, 8)].reshape(64, lanes)
             faces[2 + side] = raw_ref[7 * side]
         sum_depth(faces)
-        send_halo(turn)
 
     def fill_inner(target, raw):
         target[pl.ds(1, 6), pl.ds(8, 48)] = raw
@@ -595,7 +594,8 @@
     def operate(turn, flux, raw, target, then=None):
         outer = wide_dot(backward_outer_ref[...], flux)
         divergence(flux, raw, face_tiles, outer, outer_place)
-        send_faces(turn, raw)
+        load_faces(raw)
+        send_halo(turn)
         middle = wide_dot(backward_inner_ref[...], flux)
         ends = [(i, j) for i, j in inner_tiles if i in (3, 4)]
         rest = [(i, j) for i, j in inner_tiles if i not in (3, 4)]
@@ -615,10 +615,12 @@
         return jnp.sum(rows, axis=(0, 1), keepdims=True)
 
     fetches[0].wait()
+    load_faces(f_ref)
+    fetches[1].wait()
+    message = corner_message(f_ref[...].reshape(512, lanes))
     pl.semaphore_wait(barrier, count)
-    send_faces(0, f_ref)
-    fetches[1].wait()
-    send_y(0, corner_message(f_ref[...].reshape(512, lanes)))
+    send_halo(0)
+    send_y(0, message)
     fill_inner(base, f_ref[pl.ds(1, 6), pl.ds(8, 48)])
     fetches[2].wait()
     fetches[3].wait()

time: 33.7 us -> 33.5 us (level)
  no operation moved by 1% of the time
where the time goes in v4:
time: 33.5 us; the launch traced here: 33.3 us
  Pallas kernels  32.7 us (98%)
  between operations  0.64 us (2%)
    pallas_call x1, Pallas kernels, on_device(): pl.pallas_call(functools.partial(kernel, size_x, size_y, weights.tolist()...  30.8 us
    pallas_call x1, Pallas kernels, on_device(): pl.pallas_call(copy_kernel, out_shape=[jax.ShapeDtypeStruct(field, jnp.fl...  1.84 us

profile of v4, /device:TPU:0, one launch (start us, length us, event | category | flops | bytes accessed | tf_op | source)
XLA Modules:
  0.0 33.3 jit_solution(15439674980909492311)
XLA Ops:
  0.6 30.8 %shard_map.167 = (f32[8,64,128]{2,1,0:T(8,128)}, f32[8,64,128]{2,1,0:T(8,128)}) custom-call(f32[8,64,128]{2,1,0:T(8,128)} %bitcast.8, f32[8,512]{1,0:T(8,128)} %constant.28.clone.refs_1_, f32[8,64,128]{2,1,0:T(8,128)} %bitcast.9, f32[64,128]{1,0:T(8,128)} %constant.29.clone.refs_3_, bf16[512,512]{1,0:T(8,128)(2,1)} %constant.30.clone.refs_4_, ...), custom_call_target="tpu_custom_call" | custom-call | tf_op jit(solution)/shard_map/pallas_call | solution.py:726
  31.5 1.8 %shard_map.168 = (f32[8,64,128]{2,1,0:T(8,128)}, f32[8,64,128]{2,1,0:T(8,128)}) custom-call(f32[8,64,128]{2,1,0:T(8,128)} %get-tuple-element.6.p_in, f32[8,64,128]{2,1,0:T(8,128)} %get-tuple-element.7.r_in), custom_call_target="tpu_custom_call" | custom-call | tf_op jit(solution)/shard_map/pallas_call | solution.py:765
